TPU v7x, 256 devices: a whole 4x4x8 slice. The times are simulated.
256 devices in a mesh: wide: 32 (over x, y, core), narrow: 8 (over z).
Axes of the slice: x: 4, y: 4, z: 8, core: 2. Of those that a mesh axis runs over, the one named last changes fastest.
Arguments:
- tokens: bfloat16 [16384, 4096], P('wide', 'narrow'), may hold values from -40 to 40
- norm_gain: float32 [4096], P('narrow'), may hold values from 0.5 to 5
- w_query: bfloat16 [4096, 4096], P(None, 'narrow'), may hold values from -0.09375 to 0.09375
- key_weight: bfloat16 [4096, 1024], P(None, 'narrow'), may hold values from -0.09375 to 0.09375
- value_weight: bfloat16 [4096, 1024], P(None, 'narrow'), may hold values from -0.09375 to 0.09375
- w_out: bfloat16 [4096, 4096], P('narrow'), may hold values from -0.09375 to 0.09375
- doc_lengths: int32 [64], replicated, may hold values from 1 to 8192, 16384 in all
Outputs:
- attended: bfloat16 [16384, 4096], P('wide', 'narrow')
Inputs may be any that keep to these rules, and one draw needn't show every extreme that they name: `doc_lengths`: the lengths sum to 16384; the longest is exactly 8192.
All inputs are finite; a program needn't handle non-finite values.
Results may differ from a plain program's by a relative error of at most 0.019.
The roundings to bfloat16 on the way count: a program that leaves them out, or rounds other values in their place, can miss the bound.
Values may be sent and summed in bfloat16 or wider, within the bound.
No kernel may reach another device: no remote copies, remote signals or barrier semaphores. Data moves between devices by JAX's collectives and lax.ppermute only.
A program may use at most 128 MiB of HBM per device.

v0:
```python
import math
import jax
import jax.numpy as jnp
from jax import lax
from jax.sharding import PartitionSpec as P

MODEL_WIDTH = 4096
HEAD_SIZE = 128
EPSILON = 1e-05
ROPE_BASE = 500000.0
NEGATIVE = -1e30


def doc_of(lengths, positions):
    starts = jnp.cumsum(lengths) - lengths
    return jnp.sum((starts[None, :] <= positions[:, None]).astype(jnp.int32), axis=1) - 1


def doc_info(lengths, positions):
    starts = jnp.cumsum(lengths) - lengths
    docs = doc_of(lengths, positions)
    onehot = docs[:, None] == jnp.arange(lengths.shape[0], dtype=jnp.int32)[None, :]
    first_tok = jnp.sum(jnp.where(onehot, starts[None, :], 0), axis=1)
    return (docs, positions - first_tok)


def apply_rotary(values, rotary_positions):
    half_width = values.shape[-1] // 2
    frequency = ROPE_BASE ** (-(jnp.arange(half_width, dtype=jnp.float32) * 2.0 / values.shape[-1]))
    angles = rotary_positions.astype(jnp.float32)[:, None] * frequency[None, :]
    cosine = jnp.cos(angles)[:, None, :]
    sine_part = jnp.sin(angles)[:, None, :]
    first_half = values[..., :half_width]
    second_half = values[..., half_width:]
    return jnp.concatenate(
        [
            first_half * cosine - second_half * sine_part,
            second_half * cosine + first_half * sine_part,
        ],
        axis=-1,
    )


def per_device(tokens, norm_gain, w_query, key_weight, value_weight, w_out, doc_lengths):
    tok_rows = tokens.shape[0]
    wide_index = lax.axis_index("wide")
    as_float = tokens.astype(jnp.float32)
    squares = lax.psum(jnp.sum(as_float * as_float, axis=1), "narrow")
    inverse = lax.rsqrt(squares / MODEL_WIDTH + EPSILON)
    normed = (as_float * inverse[:, None] * norm_gain[None, :]).astype(jnp.bfloat16)
    shard_piece = lax.all_gather(normed, "narrow", axis=1, tiled=True)
    query_raw, key_unrotated, value_projected = tuple(
        (
            jnp.dot(shard_piece, matrix, preferred_element_type=jnp.float32)
            for matrix in (w_query, key_weight, value_weight)
        )
    )
    positions = wide_index * tok_rows + jnp.arange(tok_rows, dtype=jnp.int32)
    own_doc, rotary_positions = doc_info(doc_lengths, positions)
    heads_local = w_query.shape[1] // HEAD_SIZE
    kv_local = key_weight.shape[1] // HEAD_SIZE
    heads_per_group = heads_local // kv_local
    queries_own = (
        apply_rotary(query_raw.reshape(tok_rows, heads_local, HEAD_SIZE), rotary_positions)
        .astype(jnp.bfloat16)
        .reshape(tok_rows, kv_local, heads_per_group, HEAD_SIZE)
    )
    rotated_keys = apply_rotary(
        key_unrotated.reshape(tok_rows, kv_local, HEAD_SIZE), rotary_positions
    ).astype(jnp.bfloat16)
    values_cast = value_projected.reshape(tok_rows, kv_local, HEAD_SIZE).astype(jnp.bfloat16)
    key_value = jnp.stack([rotated_keys, values_cast])
    score_scale = 1.0 / math.sqrt(HEAD_SIZE)
    last_pos = jnp.max(positions)
    first_doc = jnp.min(own_doc)

    def update(carried, key_tile, value_tile, key_pos, key_doc):
        run_max, run_sum, accum = carried
        scores = (
            jnp.einsum("rkgd,nkd->kgrn", queries_own, key_tile, preferred_element_type=jnp.float32)
            * score_scale
        )
        allowed = (key_doc[None, :] == own_doc[:, None]) & (key_pos[None, :] <= positions[:, None])
        masked = jnp.where(allowed, scores, NEGATIVE)
        new_max = jnp.maximum(run_max, jnp.max(masked, axis=-1))
        weights = jnp.where(allowed, jnp.exp(scores - new_max[..., None]), 0.0)
        factor = jnp.exp(run_max - new_max)
        run_sum = run_sum * factor + jnp.sum(weights, axis=-1)
        accum = accum * factor[..., None] + jnp.einsum(
            "kgrn,nkd->kgrd",
            weights.astype(jnp.bfloat16),
            value_tile,
            preferred_element_type=jnp.float32,
        )
        return (new_max, run_sum, accum)

    start_status = (
        jnp.full((kv_local, heads_per_group, tok_rows), NEGATIVE, jnp.float32),
        jnp.zeros((kv_local, heads_per_group, tok_rows), jnp.float32),
        jnp.zeros((kv_local, heads_per_group, tok_rows, HEAD_SIZE), jnp.float32),
    )
    pair = lax.all_gather(key_value, "wide", axis=1, tiled=True)
    count_keys = pair.shape[1]
    tile_width = math.gcd(count_keys, 512)
    tile_count = count_keys // tile_width

    def tile_step(tile_index, carried_in):
        offset = tile_index * tile_width
        key_tile = lax.dynamic_slice_in_dim(pair, offset, tile_width, 1)
        key_pos = offset + jnp.arange(tile_width, dtype=jnp.int32)
        key_doc = doc_of(doc_lengths, key_pos)
        needed = (key_pos[0] <= last_pos) & (key_doc[-1] >= first_doc)
        return lax.cond(
            needed,
            lambda status: update(status, key_tile[0], key_tile[1], key_pos, key_doc),
            lambda status: status,
            carried_in,
        )

    status_now = lax.fori_loop(0, tile_count, tile_step, start_status)
    run_max, run_sum, accum = status_now
    heads_out = (
        (accum / run_sum[..., None])
        .transpose(2, 0, 1, 3)
        .reshape(tok_rows, heads_local * HEAD_SIZE)
        .astype(jnp.bfloat16)
    )
    partial_out = jnp.dot(heads_out, w_out, preferred_element_type=jnp.float32)
    return lax.psum_scatter(
        partial_out.astype(jnp.bfloat16), "narrow", scatter_dimension=1, tiled=True
    )


def solution(mesh):
    in_specs = (
        P("wide", "narrow"),
        P("narrow"),
        P(None, "narrow"),
        P(None, "narrow"),
        P(None, "narrow"),
        P("narrow", None),
        P(),
    )
    out_specs = P("wide", "narrow")
    return jax.shard_map(
        per_device, mesh=mesh, in_specs=in_specs, out_specs=out_specs, check_vma=False
    )
```

profile of v0, /device:TPU:1, one launch (start us, length us, event | category | flops | bytes accessed | tf_op | source)
XLA Modules:
  0.0 502.4 jit_solution(14981264105822187456)
XLA Ops:
  6.5 1.3 fusion.25
  7.8 17.3 %psum.7 = f32[512]{0:T(512)S(1)} all-reduce(f32[512]{0:T(512)S(1)} %fusion.25), channel_id=1, replica_groups=mesh['wide'=32,'narrow'=8] {'narrow'}, use_global_device_ids=true, to_apply=%region_1.0 | all-reduce | flops 512 | bytes 4096 | tf_op jit(solution)/shard_map/psum | solution.py:48
  25.2 2.0 fusion.27
  27.3 0.8 copy.22
  28.3 0.7 sub.52
  29.1 0.7 broadcast_add_fusion.2
  29.9 54.0 %all-gather.3.cloned.1.call-done = bf16[512,4096]{1,0:T(8,128)(2,1)} async-done(((bf16[512,512]{1,0:T(8,128)(2,1)}), bf16[512,4096]{1,0:T(8,128)(2,1)}) %all-gather.3.cloned.1.call-update) | async-done | bytes 4194320 | tf_op jit(solution)/shard_map/all_gather | solution.py:51
  83.9 3.8 convolution_bitcast_fusion
  87.7 0.6 fusion.39
  88.3 1.5 fusion.24
  89.8 0.7 pad_maximum_fusion.1
  90.8 0.7 fusion.40
  91.5 1.7 multiply_cosine_fusion
  93.2 5.8 %fusion.43 = f32[512,512]{0,1:T(8,128)S(1)} fusion(bf16[512,4096]{1,0:T(8,128)(2,1)} %all-gather.3.cloned.1.call-done, bf16[4096,512]{1,0:T(8,128)(2,1)} %param.13), kind=kOutput, calls=%fused_computation.71 | convolution fusion | flops 2147483648 | bytes 9437184 | tf_op jit(solution)/shard_map/dot_general | solution.py:54
  99.1 0.9 fusion.42
  100.3 1.4 copy.31
  101.7 1.2 fusion.28
  103.2 51.1 %all-gather.5.cloned.1.call-done = bf16[2,16384,1,128]{1,3,2,0:T(8,128)(2,1)} async-done(((bf16[2,512,1,128]{1,3,2,0:T(8,128)(2,1)}), bf16[2,16384,1,128]{1,3,2,0:T(8,128)(2,1)}) %all-gather.5.cloned.1.call-update) | async-done | bytes 8388624 | tf_op jit(solution)/shard_map/all_gather | solution.py:102
  154.3 11.9 %copy.26 = bf16[2,16384,1,128]{3,1,2,0:T(8,128)(2,1)} copy(bf16[2,16384,1,128]{1,3,2,0:T(8,128)(2,1)} %all-gather.5.cloned.1.call-done) | data formatting | bytes 16777216
  166.3 134.6 %while.20 = (s32[]{:T(128)}, f32[1,4,512]{2,1,0:T(4,128)S(1)}, f32[1,4,512]{2,1,0:T(4,128)S(1)}, f32[1,4,512,128]{3,2,1,0:T(8,128)S(1)}, s32[]{:T(128)}, /*index...) while((s32[]{:T(128)}, f32[1,4,512]{2,1,0:T(4,128)S(1)}, ...), condition=%wide.region_13.14_spmd.clone, body=%wide.region_7.13_spmd.clone.sunk | while | flops 549821440 | bytes 33448608 | solution.py:120
  166.4 0.6 slice.67
  169.9 8.8 %conditional.3 = ((f32[1,4,512]{2,1,0:T(4,128)S(1)}, f32[1,4,512]{2,1,0:T(4,128)S(1)}, f32[1,4,512,128]{3,2,1,0:T(8,128)S(1)})) conditional(s32[]{:T(128)} %convert_element_type.114, (f32[1,4,512]{2,1,0:T(4,128)S(1)}, f32[1,4,512]{2,1,0:T(4,128)S(1)}, f32[1,4,512,128]{3,2,1,0:T(8,128)S(1)}) %tuple.65, (s32[512]{0:T(512)S(1)}, s32[512]{0:T(512)S(1)}, ...), branch_computations={%region_9.9_spmd, %region_10.12_spmd} | conditional | flops 549722624 | bytes 33435770 | solution.py:113
  170.2 3.7 fusion.2
  174.0 3.8 fusion.14
  177.8 0.9 fusion.6
  178.9 0.6 slice.67
  182.4 8.8 %conditional.3 = ((f32[1,4,512]{2,1,0:T(4,128)S(1)}, f32[1,4,512]{2,1,0:T(4,128)S(1)}, f32[1,4,512,128]{3,2,1,0:T(8,128)S(1)})) conditional(s32[]{:T(128)} %convert_element_type.114, (f32[1,4,512]{2,1,0:T(4,128)S(1)}, f32[1,4,512]{2,1,0:T(4,128)S(1)}, f32[1,4,512,128]{3,2,1,0:T(8,128)S(1)}) %tuple.65, (s32[512]{0:T(512)S(1)}, s32[512]{0:T(512)S(1)}, ...), branch_computations={%region_9.9_spmd, %region_10.12_spmd} | conditional | flops 549722624 | bytes 33435770 | solution.py:113
  182.7 3.7 fusion.2
  186.5 3.8 fusion.14
  190.3 0.9 fusion.6
  191.4 0.6 slice.67
  195.1 0.6 slice.67
  202.4 0.6 slice.67
  206.0 0.6 slice.67
  209.7 0.6 slice.67
  213.3 0.6 slice.67
  217.0 0.6 slice.67
  220.6 0.6 slice.67
  228.0 0.6 slice.67
  231.6 0.6 slice.67
  235.3 0.6 slice.67
  238.9 0.6 slice.67
  242.6 0.6 slice.67
  249.9 0.6 slice.67
  300.9 1.3 copy.27
  302.2 1.4 divide_convert_fusion
  303.6 6.5 %convolution_convert_fusion = bf16[512,4096]{1,0:T(8,128)(2,1)} fusion(bf16[512,512]{0,1:T(8,128)(2,1)S(1)} %bitcast.96, bf16[512,4096]{1,0:T(8,128)(2,1)} %param.16), kind=kOutput, calls=%fused_computation.30 | convolution fusion | flops 2149580800 | bytes 8912896 | tf_op jit(solution)/shard_map/dot_general | solution.py:128
  310.1 185.8 %reduce-scatter.2.cloned.1.call-done = bf16[512,512]{1,0:T(8,128)(2,1)} async-done(((bf16[512,4096]{1,0:T(8,128)(2,1)}), bf16[512,512]{1,0:T(8,128)(2,1)}) %reduce-scatter.2.cloned.1.call-update) | async-done | bytes 524304 | tf_op jit(solution)/shard_map/reduce_scatter | solution.py:129
  (245 shorter events, 30.2 us)
Async XLA Ops:
  6.5 77.4 %copy-start = (bf16[4096,128]{1,0:T(8,128)(2,1)S(1)}, bf16[4096,128]{1,0:T(8,128)(2,1)}, u32[]{:S(2)}) copy-start(bf16[4096,128]{1,0:T(8,128)(2,1)} %param.14) | copy-start | bytes 3145732
  6.5 77.4 %all-gather.3.cloned.1.call-start = ((), (), s32[]{:S(2)}) async-start(), calls=%async_computation.1 | async-start | bytes 4718592 | tf_op jit(solution)/shard_map/all_gather | solution.py:51
  27.2 61.1 %copy-start.3 = (bf16[4096,128]{1,0:T(8,128)(2,1)S(1)}, bf16[4096,128]{1,0:T(8,128)(2,1)}, u32[]{:S(2)}) copy-start(bf16[4096,128]{1,0:T(8,128)(2,1)} %param.15) | copy-start | bytes 3145732
  27.2 127.1 %all-gather.5.cloned.1.call-start = ((), (), s32[]{:S(2)}) async-start(), calls=%async_computation.2 | async-start | bytes 8650752 | tf_op jit(solution)/shard_map/all_gather | solution.py:102
  83.9 4.4 copy-start.2
  90.6 405.3 %reduce-scatter.2.cloned.1.call-start = ((), (), s32[]{:S(2)}) async-start(), calls=%async_computation.3 | async-start | bytes 4718592 | tf_op jit(solution)/shard_map/reduce_scatter | solution.py:129
  174.0 3.8 copy-start.1
  186.5 3.8 copy-start.1
Sparse Core Ops, SparseCore 0:
  27.3 56.5 all-gather.2
  90.7 63.5 all-gather.4
  310.2 185.6 reduce-scatter.1
where the time goes:
time: 505 us; the launch traced here: 502 us
  waiting for transfers between devices  291 us (58%)
  loops' own time  80.4 us (16%)
  local copies, waits for them, and re-layouts  50.1 us (10%)
  matrix products  32.8 us (6%)
  other arithmetic  17.4 us (3%)
  blocking collectives  17.3 us (3%)
  between operations  13.2 us (3%)
    reduce_scatter x1, waiting for transfers between devices, per_device(): lax.psum_scatter(partial_out.astype(jnp.bfloat16), 'narrow', scatter_dime...  186 us
    another operation x1, loops' own time, per_device(): status_now = lax.fori_loop(0, tile_count, tile_step, start_status)  79.9 us
    all_gather x1, waiting for transfers between devices, per_device(): shard_piece = lax.all_gather(normed, 'narrow', axis=1, tiled=True)  54 us
    all_gather x1, waiting for transfers between devices, per_device(): pair = lax.all_gather(key_value, 'wide', axis=1, tiled=True)  51.1 us
    slice x64, local copies, waits for them, and re-layouts, tile_step(): needed = (key_pos[0] <= last_pos) & (key_doc[-1] >= first_doc)  33.3 us
    psum x1, blocking collectives, per_device(): squares = lax.psum(jnp.sum(as_float * as_float, axis=1), 'narrow')  17.3 us
    unnamed x9, local copies, waits for them, and re-layouts  13.6 us
    dot_general x3, matrix products, per_device(): jnp.dot(shard_piece, matrix, preferred_element_type=jnp.float32)  11.2 us
  transfers between devices with their start and end apart: 3, of which 3 were waited for; matrix products, arithmetic and copies ran while one was open for 3% of the time, Pallas kernels for 0%

commit v1 on v0

--- a/solution.py
+++ b/solution.py
@@ -9,6 +9,16 @@
 EPSILON = 1e-05
 ROPE_BASE = 500000.0
 NEGATIVE = -1e30
+
+
+def pass_along(x, mesh_axis, dim):
+    count = lax.axis_size(mesh_axis)
+    held, pieces = (x, [x])
+    for _ in range(count - 1):
+        held = lax.ppermute(held, mesh_axis, [(i, (i + 1) % count) for i in range(count)])
+        pieces.insert(0, held)
+    line = jnp.concatenate(pieces, axis=dim)
+    return jnp.roll(line, (lax.axis_index(mesh_axis) + 1) * x.shape[dim], axis=dim)
 
 
 def doc_of(lengths, positions):
@@ -48,7 +58,7 @@
     squares = lax.psum(jnp.sum(as_float * as_float, axis=1), "narrow")
     inverse = lax.rsqrt(squares / MODEL_WIDTH + EPSILON)
     normed = (as_float * inverse[:, None] * norm_gain[None, :]).astype(jnp.bfloat16)
-    shard_piece = lax.all_gather(normed, "narrow", axis=1, tiled=True)
+    shard_piece = pass_along(normed, "narrow", 1)
     query_raw, key_unrotated, value_projected = tuple(
         (
             jnp.dot(shard_piece, matrix, preferred_element_type=jnp.float32)

time: 505 us -> 555 us (1.099)
  waiting for transfers between devices: 291 us -> 331 us
  local copies, waits for them, and re-layouts: 50.1 us -> 57 us
    ppermute x0 -> x7, waiting for transfers between devices: none -> 83 us  [pass_along(): lax.ppermute(held, mesh_axis, [(i, (i + 1) % count) for i in range(count)])]
    all_gather x1 -> x0, waiting for transfers between devices: 54 us -> none  [per_device(): shard_piece = lax.all_gather(normed, 'narrow', axis=1, tiled=True)]
    all_gather x1, waiting for transfers between devices: 51.1 us -> 62.3 us  [per_device(): pair = lax.all_gather(key_value, 'wide', axis=1, tiled=True)]
    unnamed x9 -> x31, local copies, waits for them, and re-layouts: 13.6 us -> 20.6 us
  transfers between devices with their start and end apart: 3 -> 9, of which waited for: 3 -> 9; matrix products, arithmetic and copies ran while one was open for 3% -> 3% of each run, Pallas kernels for 0% -> 0%
where the time goes in v1:
time: 555 us; the launch traced here: 550 us
  waiting for transfers between devices  331 us (60%)
  loops' own time  83.1 us (15%)
  local copies, waits for them, and re-layouts  57 us (10%)
  matrix products  30.5 us (5%)
  blocking collectives  17.3 us (3%)
  other arithmetic  17.1 us (3%)
  between operations  13.7 us (2%)
    reduce_scatter x1, waiting for transfers between devices, per_device(): lax.psum_scatter(partial_out.astype(jnp.bfloat16), 'narrow', scatter_dime...  186 us
    ppermute x7, waiting for transfers between devices, pass_along(): lax.ppermute(held, mesh_axis, [(i, (i + 1) % count) for i in range(count)])  83 us
    another operation x1, loops' own time, per_device(): status_now = lax.fori_loop(0, tile_count, tile_step, start_status)  82.6 us
    all_gather x1, waiting for transfers between devices, per_device(): pair = lax.all_gather(key_value, 'wide', axis=1, tiled=True)  62.3 us
    slice x64, local copies, waits for them, and re-layouts, tile_step(): needed = (key_pos[0] <= last_pos) & (key_doc[-1] >= first_doc)  33.3 us
    unnamed x31, local copies, waits for them, and re-layouts  20.6 us
    psum x1, blocking collectives, per_device(): squares = lax.psum(jnp.sum(as_float * as_float, axis=1), 'narrow')  17.3 us
  transfers between devices with their start and end apart: 9, of which 9 were waited for; matrix products, arithmetic and copies ran while one was open for 3% of the time, Pallas kernels for 0%

profile of v1, /device:TPU:1, one launch (start us, length us, event | category | flops | bytes accessed | tf_op | source)
XLA Modules:
  0.0 550.1 jit_solution(17790930764973695096)
XLA Ops:
  6.5 1.3 fusion.39
  7.9 17.3 %psum.7 = f32[512]{0:T(512)S(1)} all-reduce(f32[512]{0:T(512)S(1)} %fusion.39), channel_id=1, replica_groups=mesh['wide'=32,'narrow'=8] {'narrow'}, use_global_device_ids=true, to_apply=%region_1.0 | all-reduce | flops 512 | bytes 4096 | tf_op jit(solution)/shard_map/psum | solution.py:58
  25.2 1.2 fusion.41
  26.5 10.4 %collective-permute-done = bf16[512,512]{1,0:T(8,128)(2,1)S(1)} collective-permute-done((bf16[512,512]{1,0:T(8,128)(2,1)S(1)}, bf16[512,512]{1,0:T(8,128)(2,1)S(1)}, u32[]{:S(2)}, u32[]{:S(2)}) %collective-permute-start) | collective-permute-done | bytes 524320 | tf_op jit(solution)/shard_map/ppermute | solution.py:18
  36.9 10.4 %collective-permute-done.1 = bf16[512,512]{1,0:T(8,128)(2,1)S(1)} collective-permute-done((bf16[512,512]{1,0:T(8,128)(2,1)S(1)}, bf16[512,512]{1,0:T(8,128)(2,1)S(1)}, u32[]{:S(2)}, u32[]{:S(2)}) %collective-permute-start.1) | collective-permute-done | bytes 524320 | tf_op jit(solution)/shard_map/ppermute | solution.py:18
  47.3 10.9 %collective-permute-done.2 = bf16[512,512]{1,0:T(8,128)(2,1)S(1)} collective-permute-done((bf16[512,512]{1,0:T(8,128)(2,1)S(1)}, bf16[512,512]{1,0:T(8,128)(2,1)S(1)}, u32[]{:S(2)}, u32[]{:S(2)}) %collective-permute-start.2) | collective-permute-done | bytes 524320 | tf_op jit(solution)/shard_map/ppermute | solution.py:18
  58.2 12.0 %collective-permute-done.3 = bf16[512,512]{1,0:T(8,128)(2,1)S(1)} collective-permute-done((bf16[512,512]{1,0:T(8,128)(2,1)S(1)}, bf16[512,512]{1,0:T(8,128)(2,1)S(1)}, u32[]{:S(2)}, u32[]{:S(2)}) %collective-permute-start.3) | collective-permute-done | bytes 524320 | tf_op jit(solution)/shard_map/ppermute | solution.py:18
  70.2 0.8 copy-done.3
  71.0 12.4 %collective-permute-done.4 = bf16[512,512]{1,0:T(8,128)(2,1)} collective-permute-done((bf16[512,512]{1,0:T(8,128)(2,1)S(1)}, bf16[512,512]{1,0:T(8,128)(2,1)}, u32[]{:S(2)}, u32[]{:S(2)}) %collective-permute-start.4) | collective-permute-done | bytes 524320 | tf_op jit(solution)/shard_map/ppermute | solution.py:18
  83.4 0.7 copy.22
  84.4 0.7 sub.56
  85.1 12.4 %collective-permute-done.5 = bf16[512,512]{1,0:T(8,128)(2,1)} collective-permute-done((bf16[512,512]{1,0:T(8,128)(2,1)}, bf16[512,512]{1,0:T(8,128)(2,1)}, u32[]{:S(2)}, u32[]{:S(2)}) %collective-permute-start.5) | collective-permute-done | bytes 524320 | tf_op jit(solution)/shard_map/ppermute | solution.py:18
  97.6 0.7 broadcast_add_fusion.2
  98.4 14.5 %collective-permute-done.6 = bf16[512,512]{1,0:T(8,128)(2,1)S(1)} collective-permute-done((bf16[512,512]{1,0:T(8,128)(2,1)}, bf16[512,512]{1,0:T(8,128)(2,1)S(1)}, u32[]{:S(2)}, u32[]{:S(2)}) %collective-permute-start.6) | collective-permute-done | bytes 524320 | tf_op jit(solution)/shard_map/ppermute | solution.py:18
  113.0 1.1 constant_dynamic-update-slice_fusion.14
  114.1 1.1 constant_dynamic-update-slice_fusion.13
  115.2 1.1 constant_dynamic-update-slice_fusion.12
  116.8 1.1 constant_dynamic-update-slice_fusion.6
  118.0 1.1 constant_dynamic-update-slice_fusion.5
  119.6 1.5 fusion.30
  121.2 1.5 fusion.36
  122.7 0.6 fusion.53
  123.3 0.7 pad_maximum_fusion.1
  124.3 0.7 fusion.54
  125.0 1.7 multiply_cosine_fusion
  126.7 5.8 %fusion.24 = f32[512,512]{0,1:T(8,128)S(1)} fusion(bf16[4096,512]{1,0:T(8,128)(2,1)} %param.13, bf16[512,8192]{1,0:T(8,128)(2,1)} %copy-done.5, s32[]{:T(128)S(6)} %select_n.37), kind=kOutput, calls=%fused_computation.31 | convolution fusion | flops 2147483648 | bytes 9437188 | tf_op jit(solution)/shard_map/dot_general | solution.py:64
  132.6 0.9 fusion.59
  133.8 1.4 copy.31
  135.2 1.2 fusion.42
  136.7 62.3 %all-gather.2.cloned.1.call-done = bf16[2,16384,1,128]{1,3,2,0:T(8,128)(2,1)} async-done(((bf16[2,512,1,128]{1,3,2,0:T(8,128)(2,1)}), bf16[2,16384,1,128]{1,3,2,0:T(8,128)(2,1)}) %all-gather.2.cloned.1.call-update) | async-done | bytes 8388624 | tf_op jit(solution)/shard_map/all_gather | solution.py:112
  199.0 11.9 %copy.26 = bf16[2,16384,1,128]{3,1,2,0:T(8,128)(2,1)} copy(bf16[2,16384,1,128]{1,3,2,0:T(8,128)(2,1)} %all-gather.2.cloned.1.call-done) | data formatting | bytes 16777216
  211.0 137.3 %while.20 = (s32[]{:T(128)}, f32[1,4,512]{2,1,0:T(4,128)S(1)}, f32[1,4,512]{2,1,0:T(4,128)S(1)}, f32[1,4,512,128]{3,2,1,0:T(8,128)S(1)}, s32[]{:T(128)}, /*index...) while((s32[]{:T(128)}, f32[1,4,512]{2,1,0:T(4,128)S(1)}, ...), condition=%wide.region_13.14_spmd.clone, body=%wide.region_7.13_spmd.clone.sunk | while | flops 549821440 | bytes 33448608 | solution.py:130
  211.1 0.6 slice.67
  214.7 8.9 %conditional.3 = ((f32[1,4,512]{2,1,0:T(4,128)S(1)}, f32[1,4,512]{2,1,0:T(4,128)S(1)}, f32[1,4,512,128]{3,2,1,0:T(8,128)S(1)})) conditional(s32[]{:T(128)} %convert_element_type.122, (f32[1,4,512]{2,1,0:T(4,128)S(1)}, f32[1,4,512]{2,1,0:T(4,128)S(1)}, f32[1,4,512,128]{3,2,1,0:T(8,128)S(1)}) %tuple.65, (s32[512]{0:T(512)S(1)}, s32[512]{0:T(512)S(1)}, ...), branch_computations={%region_9.9_spmd, %region_10.12_spmd} | conditional | flops 549722624 | bytes 33435770 | solution.py:123
  215.0 3.7 fusion.2
  218.8 3.8 fusion.14
  222.6 0.9 fusion.6
  223.7 0.6 slice.67
  227.3 8.8 %conditional.3 = ((f32[1,4,512]{2,1,0:T(4,128)S(1)}, f32[1,4,512]{2,1,0:T(4,128)S(1)}, f32[1,4,512,128]{3,2,1,0:T(8,128)S(1)})) conditional(s32[]{:T(128)} %convert_element_type.122, (f32[1,4,512]{2,1,0:T(4,128)S(1)}, f32[1,4,512]{2,1,0:T(4,128)S(1)}, f32[1,4,512,128]{3,2,1,0:T(8,128)S(1)}) %tuple.65, (s32[512]{0:T(512)S(1)}, s32[512]{0:T(512)S(1)}, ...), branch_computations={%region_9.9_spmd, %region_10.12_spmd} | conditional | flops 549722624 | bytes 33435770 | solution.py:123
  227.6 3.7 fusion.2
  231.4 3.8 fusion.14
  235.2 0.9 fusion.6
  236.3 0.6 slice.67
  240.0 0.6 slice.67
  348.3 1.3 copy.27
  349.6 1.4 divide_convert_fusion
  351.0 6.5 %convolution_convert_fusion = bf16[512,4096]{1,0:T(8,128)(2,1)} fusion(bf16[512,512]{0,1:T(8,128)(2,1)S(1)} %bitcast.93, bf16[512,4096]{1,0:T(8,128)(2,1)} %param.16), kind=kOutput, calls=%fused_computation.30 | convolution fusion | flops 2149580800 | bytes 8912896 | tf_op jit(solution)/shard_map/dot_general | solution.py:138
  357.5 185.8 %reduce-scatter.2.cloned.1.call-done = bf16[512,512]{1,0:T(8,128)(2,1)} async-done(((bf16[512,4096]{1,0:T(8,128)(2,1)}), bf16[512,512]{1,0:T(8,128)(2,1)}) %reduce-scatter.2.cloned.1.call-update) | async-done | bytes 524304 | tf_op jit(solution)/shard_map/reduce_scatter | solution.py:139
  (280 shorter events, 37.9 us)
Async XLA Ops:
  6.5 113.1 %copy-start = (bf16[4096,128]{1,0:T(8,128)(2,1)S(1)}, bf16[4096,128]{1,0:T(8,128)(2,1)}, u32[]{:S(2)}) copy-start(bf16[4096,128]{1,0:T(8,128)(2,1)} %param.14) | copy-start | bytes 3145732
  6.5 110.0 %copy-start.2 = (bf16[512,512]{1,0:T(8,128)(2,1)S(1)}, bf16[512,512]{1,0:T(8,128)(2,1)}, u32[]{:S(2)}) copy-start(bf16[512,512]{1,0:T(8,128)(2,1)} %param.11) | copy-start | bytes 1572868
  6.5 110.0 %copy-start.6 = (f32[512]{0:T(512)S(1)}, f32[512]{0:T(512)}, u32[]{:S(2)}) copy-start(f32[512]{0:T(512)} %param.12) | copy-start | bytes 6148
  6.5 192.4 %all-gather.2.cloned.1.call-start = ((), (), s32[]{:S(2)}) async-start(), calls=%async_computation.1 | async-start | bytes 8650752 | tf_op jit(solution)/shard_map/all_gather | solution.py:112
  26.4 10.5 %collective-permute-start = (bf16[512,512]{1,0:T(8,128)(2,1)S(1)}, bf16[512,512]{1,0:T(8,128)(2,1)S(1)}, u32[]{:S(2)}, u32[]{:S(2)}) collective-permute-start(bf16[512,512]{1,0:T(8,128)(2,1)S(1)} %fusion.41), channel_id=1, source_target_pairs={{0,1},{1,2},{2,3},{3,4},{4,5},{5,6},{6,7},{7,0},{8,9},{9,10},{10,1... | collective-permute-start | bytes 1572872 | tf_op jit(solution)/shard_map/ppermute | solution.py:18
  36.9 10.4 %collective-permute-start.1 = (bf16[512,512]{1,0:T(8,128)(2,1)S(1)}, bf16[512,512]{1,0:T(8,128)(2,1)S(1)}, u32[]{:S(2)}, u32[]{:S(2)}) collective-permute-start(bf16[512,512]{1,0:T(8,128)(2,1)S(1)} %collective-permute-done), channel_id=1, source_target_pairs={{0,1},{1,2},{2,3},{3,4},{4,5},{5,6},{6,7},{7,0},{8,9},{9,10},{10,1... | collective-permute-start | bytes 1572872 | tf_op jit(solution)/shard_map/ppermute | solution.py:18
  47.3 10.9 %collective-permute-start.2 = (bf16[512,512]{1,0:T(8,128)(2,1)S(1)}, bf16[512,512]{1,0:T(8,128)(2,1)S(1)}, u32[]{:S(2)}, u32[]{:S(2)}) collective-permute-start(bf16[512,512]{1,0:T(8,128)(2,1)S(1)} %collective-permute-done.1), channel_id=1, source_target_pairs={{0,1},{1,2},{2,3},{3,4},{4,5},{5,6},{6,7},{7,0},{8,9},{9,10},{10,1... | collective-permute-start | bytes 1572872 | tf_op jit(solution)/shard_map/ppermute | solution.py:18
  58.2 12.0 %collective-permute-start.3 = (bf16[512,512]{1,0:T(8,128)(2,1)S(1)}, bf16[512,512]{1,0:T(8,128)(2,1)S(1)}, u32[]{:S(2)}, u32[]{:S(2)}) collective-permute-start(bf16[512,512]{1,0:T(8,128)(2,1)S(1)} %collective-permute-done.2), channel_id=1, source_target_pairs={{0,1},{1,2},{2,3},{3,4},{4,5},{5,6},{6,7},{7,0},{8,9},{9,10},{10,1... | collective-permute-start | bytes 1572872 | tf_op jit(solution)/shard_map/ppermute | solution.py:18
  70.2 0.8 copy-start.3
  71.0 12.4 %collective-permute-start.4 = (bf16[512,512]{1,0:T(8,128)(2,1)S(1)}, bf16[512,512]{1,0:T(8,128)(2,1)}, u32[]{:S(2)}, u32[]{:S(2)}) collective-permute-start(bf16[512,512]{1,0:T(8,128)(2,1)S(1)} %collective-permute-done.3), channel_id=1, source_target_pairs={{0,1},{1,2},{2,3},{3,4},{4,5},{5,6},{6,7},{7,0},{8,9},{9,10},{10,1... | collective-permute-start | bytes 1572872 | tf_op jit(solution)/shard_map/ppermute | solution.py:18
  83.4 14.2 %collective-permute-start.5 = (bf16[512,512]{1,0:T(8,128)(2,1)}, bf16[512,512]{1,0:T(8,128)(2,1)}, u32[]{:S(2)}, u32[]{:S(2)}) collective-permute-start(bf16[512,512]{1,0:T(8,128)(2,1)} %collective-permute-done.4), channel_id=1, source_target_pairs={{0,1},{1,2},{2,3},{3,4},{4,5},{5,6},{6,7},{7,0},{8,9},{9,10},{10,1... | collective-permute-start | bytes 1572872 | tf_op jit(solution)/shard_map/ppermute | solution.py:18
  85.0 34.1 %copy-start.4 = (bf16[512,512]{1,0:T(8,128)(2,1)S(1)}, bf16[512,512]{1,0:T(8,128)(2,1)}, u32[]{:S(2)}) copy-start(bf16[512,512]{1,0:T(8,128)(2,1)} %copy-done.3) | copy-start | bytes 1572868
  97.6 15.3 %collective-permute-start.6 = (bf16[512,512]{1,0:T(8,128)(2,1)}, bf16[512,512]{1,0:T(8,128)(2,1)S(1)}, u32[]{:S(2)}, u32[]{:S(2)}) collective-permute-start(bf16[512,512]{1,0:T(8,128)(2,1)} %collective-permute-done.5), channel_id=1, source_target_pairs={{0,1},{1,2},{2,3},{3,4},{4,5},{5,6},{6,7},{7,0},{8,9},{9,10},{10,1... | collective-permute-start | bytes 1572872 | tf_op jit(solution)/shard_map/ppermute | solution.py:18
  116.5 4.7 copy-start.7
  119.6 3.7 copy-start.5
  124.0 419.3 %reduce-scatter.2.cloned.1.call-start = ((), (), s32[]{:S(2)}) async-start(), calls=%async_computation.2 | async-start | bytes 4718592 | tf_op jit(solution)/shard_map/reduce_scatter | solution.py:139
  218.8 3.8 copy-start.1
  231.4 3.8 copy-start.1
Sparse Core Ops, SparseCore 0:
  124.2 74.7 all-gather.1
  357.6 185.6 reduce-scatter.1
